TPU v7x, 32 devices: a whole 2x2x4 slice. The times are simulated.
32 devices in a mesh: rows: 2 (over x), bx: 4 (over y, core), by: 4 (over z).
Axes of the slice: x: 2, y: 2, z: 4, core: 2. Of those that a mesh axis runs over, the one named last changes fastest.
Arguments:
- pair_mult: bfloat16 [131072, 256], P(('rows', 'bx', 'by')), may hold values from -1.5 to 1.5
- pair_dens: float32 [131072], P(('rows', 'bx', 'by')), may hold values from -3 to 3
- pair_live: int32 [131072], P(('rows', 'bx', 'by')), may hold values 0 or 1
- pair_box: int32 [131072], P(('rows', 'bx', 'by')), may hold values from 0 to 767
- inter_mask: int32 [16, 32, 32, 98], P('rows', 'bx', 'by'), may hold values 0 or 1
- row_scale: float32 [98, 256], replicated, may hold values from 0.3 to 1.5
- col_scale: float32 [98, 256], replicated, may hold values from 0.3 to 1.5
- base: bfloat16 [256, 256], replicated, may hold values from -0.0390625 to 0.0390625
- lattice: float32 [256, 256], replicated, may hold values from -0.0029296875 to 0.0029296875
Outputs:
- box_locals: bfloat16 [16, 32, 32, 256], P('rows', 'bx', 'by')
- pair_j: float32 [131072], P(('rows', 'bx', 'by'))
Inputs may be any that keep to these rules, and one draw needn't show every extreme that they name: `pair_box`: numbers a box of the pair's own x, y slab as (l * 8 + x) * 8 + y with l in 0..11, x in 0..7, y in 0..7, where level l is the box z = (rows index of the device * 8 + l - 2) mod 16.
All inputs are finite; a program needn't handle non-finite values. No bound on the sum of `pair_live` or of `inter_mask` on one device may be relied on, other than what follows from the above.
Results may differ from a plain program's by a relative error of at most 0.007.
Values may be sent and summed in bfloat16 or wider, within the bound.
A program may use at most 128 MiB of HBM per device.

v0:
```python
import functools

import jax
import jax.numpy as jnp
from jax import lax
from jax.experimental import pallas as pl
from jax.experimental.pallas import tpu as pltpu
from jax.sharding import PartitionSpec as P

PAIR_CHUNK = 512
VMEM = pl.BlockSpec(memory_space=pltpu.VMEM)


def offset_table():
    listed = []
    for shift_z in range(-2, 3):
        for shift_x in range(-2, 3):
            for shift_y in range(-2, 3):
                if max(abs(shift_z), abs(shift_x), abs(shift_y)) == 2:
                    listed.append((shift_z, shift_x, shift_y))
    return listed


def moments_kernel(mult_ref, dens_ref, live_ref, box_ref, near_ref, cell_ref):
    near = near_ref.shape[0]
    labels = lax.broadcasted_iota(jnp.int32, (near, PAIR_CHUNK), 0)
    near_ref[...] = jnp.zeros_like(near_ref)

    def step(index, carry):
        at = pl.ds(pl.multiple_of(index * PAIR_CHUNK, PAIR_CHUNK), PAIR_CHUNK)
        weight = dens_ref[:, at] * live_ref[:, at].astype(jnp.float32)
        selector = jnp.where(labels == box_ref[:, at], weight, 0.0).astype(jnp.bfloat16)
        near_ref[...] += jnp.dot(selector, mult_ref[at, :], preferred_element_type=jnp.float32)
        return carry

    lax.fori_loop(0, mult_ref.shape[0] // PAIR_CHUNK, step, 0)
    cell_ref[...] = jnp.sum(near_ref[...], 0, keepdims=True)


def pairs_kernel(locals_ref, mult_ref, box_ref, out_ref):
    near = locals_ref.shape[0]
    labels = lax.broadcasted_iota(jnp.int32, (near, PAIR_CHUNK), 0)

    def step(index, carry):
        at = pl.ds(pl.multiple_of(index * PAIR_CHUNK, PAIR_CHUNK), PAIR_CHUNK)
        values = lax.dot_general(
            locals_ref[...],
            mult_ref[at, :],
            (((1,), (1,)), ((), ())),
            preferred_element_type=jnp.float32,
        )
        hits = jnp.where(labels == box_ref[:, at], values, 0.0)
        out_ref[:, at] = jnp.sum(hits, 0, keepdims=True)
        return carry

    lax.fori_loop(0, mult_ref.shape[0] // PAIR_CHUNK, step, 0)


def expand_operators(rows_ref, cols_ref, base_ref, wide_ref):
    offsets, comps, outs = wide_ref.shape

    def step(index, carry):
        at = pl.ds(pl.multiple_of(index * 16, 16), 16)
        core = base_ref[at, :].astype(jnp.float32)
        rows = rows_ref[at, :]
        for entry in range(offsets):
            scaled = core * rows[:, entry : entry + 1] * cols_ref[entry : entry + 1, :]
            wide_ref[entry, at, :] = scaled.astype(jnp.bfloat16)
        return carry

    lax.fori_loop(0, comps // 16, step, 0)


def expand_masks(mask_ref, wide_ref):
    offsets, boxes, lanes = wide_ref.shape

    def step(index, carry):
        at = pl.ds(pl.multiple_of(index * 32, 32), 32)
        gates = mask_ref[at, :].astype(jnp.float32)
        for entry in range(offsets):
            wide = jnp.broadcast_to(gates[:, entry : entry + 1], (32, lanes))
            wide_ref[entry, at, :] = wide.astype(jnp.bfloat16)
        return carry

    lax.fori_loop(0, boxes // 32, step, 0)


def shifted_copies(padded_ref, shifted_ref):
    depth = padded_ref.shape[0]
    size_y = padded_ref.shape[2] - 4
    spread_x = padded_ref.shape[1]
    comps = padded_ref.shape[3]

    def step(level, carry):
        for move in range(5):
            part = padded_ref[level, :, move : move + size_y, :].astype(jnp.bfloat16)
            shifted_ref[move, 0, level] = part.reshape(spread_x * size_y, comps)
            part = padded_ref[level, 1 : spread_x - 1, move : move + size_y, :].astype(jnp.bfloat16)
            shifted_ref[move, 1, level, : (spread_x - 2) * size_y] = part.reshape(
                (spread_x - 2) * size_y, comps
            )
        return carry

    lax.fori_loop(0, depth, step, 0)


def far_field(shifted_ref, gates_ref, wide_ref, total_ref, left_ref, sizes):
    size_z, size_x, size_y = sizes
    rows = size_x * size_y
    boxes = size_z * rows
    comps = wide_ref.shape[1]

    def group(shift_z, shift_x, first, moves):
        even = (shift_x + 2) % 2
        start = pl.multiple_of(((shift_x + 2) // 2) * 2 * size_y, 2 * size_y)
        for place, move in enumerate(moves):
            source = shifted_ref[move + 2, even, pl.ds(shift_z + 2, size_z), pl.ds(start, rows), :]
            source = source.reshape(boxes, comps)
            gate = gates_ref[first + place]
            for half in range(comps // 128):
                lanes = slice(half * 128, half * 128 + 128)
                left_ref[:, place * comps + half * 128 : place * comps + half * 128 + 128] = (
                    source[:, lanes] * gate
                )
        count = len(moves)
        operator = wide_ref[pl.ds(first, count)].reshape(count * comps, comps)
        total_ref[...] += jnp.dot(
            left_ref[:, : count * comps], operator, preferred_element_type=jnp.float32
        )

    def outer(index, carry):
        side, spot = index // 5, index % 5
        group(side * 4 - 2, spot - 2, side * 73 + spot * 5, (-2, -1, 0, 1, 2))
        return carry

    def edge(index, carry):
        level, side = index // 2, index % 2
        group(level - 1, side * 4 - 2, 25 + level * 16 + side * 11, (-2, -1, 0, 1, 2))
        return carry

    def inner(index, carry):
        level, spot = index // 3, index % 3
        group(level - 1, spot - 1, 30 + level * 16 + spot * 2, (-2, 2))
        return carry

    lax.fori_loop(0, 10, outer, 0)
    lax.fori_loop(0, 6, edge, 0)
    lax.fori_loop(0, 9, inner, 0)


def field_kernel(
    sizes, padded_ref, mask_ref, rows_ref, cols_ref, base_ref, term_ref, out_ref,
    gates_ref, wide_ref, shifted_ref, left_ref, total_ref,
):
    expand_operators(rows_ref, cols_ref, base_ref, wide_ref)
    expand_masks(mask_ref, gates_ref)
    shifted_copies(padded_ref, shifted_ref)
    total_ref[...] = jnp.broadcast_to(term_ref[...], total_ref.shape)
    far_field(shifted_ref, gates_ref, wide_ref, total_ref, left_ref, sizes)
    out_ref[...] = total_ref[...].astype(jnp.bfloat16)


def ring(axis):
    count = lax.axis_size(axis)
    up = [(i, (i + 1) % count) for i in range(count)]
    return up, [(j, i) for i, j in up]


def padded_2(x, axis, dim):
    up, down = ring(axis)
    length = x.shape[dim]
    before = lax.ppermute(lax.slice_in_dim(x, length - 2, length, axis=dim), axis, up)
    after = lax.ppermute(lax.slice_in_dim(x, 0, 2, axis=dim), axis, down)
    return jnp.concatenate([before, x, after], axis=dim)


def per_device(
    pair_mult, pair_dens, pair_live, pair_box, inter_mask, row_scale, col_scale, base, lattice
):
    pairs, comps = pair_mult.shape
    depth, width_x, width_y, offsets = inter_mask.shape
    boxes = depth * width_x * width_y
    near = (depth + 4) * width_x * width_y
    box_row = pair_box.reshape(1, pairs)
    params = pltpu.CompilerParams(vmem_limit_bytes=56 * 1024 * 1024)
    partial, cell_part = pl.pallas_call(
        moments_kernel,
        out_shape=(
            jax.ShapeDtypeStruct((near, comps), jnp.float32),
            jax.ShapeDtypeStruct((1, comps), jnp.float32),
        ),
        in_specs=[VMEM] * 4,
        out_specs=(VMEM, VMEM),
        compiler_params=params,
    )(pair_mult, pair_dens.reshape(1, pairs), pair_live.reshape(1, pairs), box_row)
    cell = lax.psum(cell_part, ("rows", "bx", "by"))
    term = jnp.dot(cell, lattice, precision=lax.Precision.HIGHEST)

    partial = partial.reshape(depth + 4, width_x, width_y, comps)
    up, down = ring("rows")
    low = lax.ppermute(partial[depth:].astype(jnp.bfloat16), "rows", up)
    high = lax.ppermute(partial[:4].astype(jnp.bfloat16), "rows", down)
    full = jnp.concatenate(
        [
            partial[:4] + low.astype(jnp.float32),
            partial[4:depth],
            partial[depth:] + high.astype(jnp.float32),
        ],
        axis=0,
    ).astype(jnp.bfloat16)
    padded = padded_2(padded_2(full, "bx", 1), "by", 2).astype(jnp.float32)

    box_locals = pl.pallas_call(
        functools.partial(field_kernel, (depth, width_x, width_y)),
        out_shape=jax.ShapeDtypeStruct((boxes, comps), jnp.bfloat16),
        in_specs=[VMEM] * 6,
        out_specs=VMEM,
        scratch_shapes=[
            pltpu.VMEM((offsets, boxes, 128), jnp.bfloat16),
            pltpu.VMEM((offsets, comps, comps), jnp.bfloat16),
            pltpu.VMEM((5, 2, depth + 4, (width_x + 4) * width_y, comps), jnp.bfloat16),
            pltpu.VMEM((boxes, 5 * comps), jnp.bfloat16),
            pltpu.VMEM((boxes, comps), jnp.float32),
        ],
        compiler_params=params,
    )(padded, inter_mask.reshape(boxes, offsets), row_scale.T, col_scale, base, term)

    box_locals = box_locals.reshape(depth, width_x, width_y, comps)
    near_locals = padded_2(box_locals, "rows", 0).reshape(near, comps)
    pair_j = pl.pallas_call(
        pairs_kernel,
        out_shape=jax.ShapeDtypeStruct((1, pairs), jnp.float32),
        in_specs=[VMEM] * 3,
        out_specs=VMEM,
        compiler_params=params,
    )(near_locals, pair_mult, box_row)
    return (box_locals, pair_j.reshape(pairs))


def solution(mesh):
    return jax.shard_map(
        per_device,
        mesh=mesh,
        in_specs=(
            P(("rows", "bx", "by"), None),
            P(("rows", "bx", "by")),
            P(("rows", "bx", "by")),
            P(("rows", "bx", "by")),
            P("rows", "bx", "by", None),
            P(),
            P(),
            P(),
            P(),
        ),
        out_specs=(P("rows", "bx", "by", None), P(("rows", "bx", "by"))),
        check_vma=False,
    )
```

profile of v0, /device:TPU:0, one launch (start us, length us, event | category | flops | bytes accessed | tf_op | source)
XLA Modules:
  0.0 113.6 jit_solution(6457882879279109638)
XLA Ops:
  0.6 5.6 %shard_map.104 = (f32[768,256]{1,0:T(8,128)}, f32[1,256]{1,0:T(1,128)}) custom-call(bf16[4096,256]{1,0:T(8,128)(2,1)} %mult_ref.3, f32[1,4096]{1,0:T(1,128)} %bitcast.34, s32[1,4096]{1,0:T(1,128)} %bitcast.35, s32[1,4096]{1,0:T(1,128)} %bitcast.30), custom_call_target="tpu_custom_call" | custom-call | tf_op jit(solution)/shard_map/pallas_call | solution.py:186
  6.2 1.1 fusion
  7.4 3.0 %collective-permute-start = (bf16[4,8,8,256]{3,2,1,0:T(8,128)(2,1)S(1)}, bf16[4,8,8,256]{3,2,1,0:T(8,128)(2,1)S(1)}, u32[]{:S(2)}, u32[]{:S(2)}) collective-permute-start(bf16[4,8,8,256]{3,2,1,0:T(8,128)(2,1)S(1)} %convert_element_type.16), channel_id=1, source_target_pairs={{0,16},{16,0},{1,17},{17,1},{2,18},{18,2},{3,19},{19,3},{4,20},{20... | collective-permute-start | bytes 393224 | tf_op jit(solution)/shard_map/ppermute | solution.py:201
  10.5 1.0 slice.63
  11.4 3.3 %collective-permute-done = bf16[4,8,8,256]{3,2,1,0:T(8,128)(2,1)S(1)} collective-permute-done((bf16[4,8,8,256]{3,2,1,0:T(8,128)(2,1)S(1)}, bf16[4,8,8,256]{3,2,1,0:T(8,128)(2,1)S(1)}, u32[]{:S(2)}, u32[]{:S(2)}) %collective-permute-start) | collective-permute-done | bytes 131104 | tf_op jit(solution)/shard_map/ppermute | solution.py:201
  14.7 1.9 %collective-permute-done.1 = bf16[4,8,8,256]{3,2,1,0:T(8,128)(2,1)S(1)} collective-permute-done((bf16[4,8,8,256]{3,2,1,0:T(8,128)(2,1)S(1)}, bf16[4,8,8,256]{3,2,1,0:T(8,128)(2,1)S(1)}, u32[]{:S(2)}, u32[]{:S(2)}) %collective-permute-start.1) | collective-permute-done | bytes 131104 | tf_op jit(solution)/shard_map/ppermute | solution.py:202
  16.8 1.7 %collective-permute-start.3 = (bf16[12,2,8,256]{3,2,1,0:T(8,128)(2,1)S(1)}, bf16[12,2,8,256]{3,2,1,0:T(8,128)(2,1)S(1)}, u32[]{:S(2)}, u32[]{:S(2)}) collective-permute-start(bf16[12,2,8,256]{3,2,1,0:T(8,128)(2,1)S(1)} %get-tuple-element.11), channel_id=1, source_target_pairs={{4,0},{8,4},{12,8},{0,12},{5,1},{9,5},{13,9},{1,13},{6,2},{10,6},{... | collective-permute-start | bytes 294920 | tf_op jit(solution)/shard_map/ppermute | solution.py:173
  18.5 0.7 copy.11
  19.3 40.8 %psum.7 = f32[256]{0:T(256)S(1)} all-reduce(f32[256]{0:T(256)S(1)} %bitcast.38), channel_id=1, replica_groups=mesh['rows'=2,'bx'=4,'by'=4] {'rows','bx','by'}, use_global_device_ids=true, to_apply=%region_0.0 | all-reduce | flops 256 | bytes 2048 | tf_op jit(solution)/shard_map/psum | solution.py:196
  60.0 0.2 pad_maximum_fusion.5
  60.2 1.6 %collective-permute-start.4 = (bf16[12,12,2,256]{3,2,1,0:T(2,128)(2,1)S(1)}, bf16[12,12,2,256]{3,2,1,0:T(2,128)(2,1)S(1)}, u32[]{:S(2)}, u32[]{:S(2)}) collective-permute-start(bf16[12,12,2,256]{3,2,1,0:T(2,128)(2,1)S(1)} %get-tuple-element.8), channel_id=1, source_target_pairs={{0,1},{1,2},{2,3},{3,0},{4,5},{5,6},{6,7},{7,4},{8,9},{9,10},{10,1... | collective-permute-start | bytes 442376 | tf_op jit(solution)/shard_map/ppermute | solution.py:172
  61.8 2.3 %collective-permute-start.5 = (bf16[12,12,2,256]{3,2,1,0:T(2,128)(2,1)S(1)}, bf16[12,12,2,256]{3,2,1,0:T(2,128)(2,1)S(1)}, u32[]{:S(2)}, u32[]{:S(2)}) collective-permute-start(bf16[12,12,2,256]{3,2,1,0:T(2,128)(2,1)S(1)} %get-tuple-element.9), channel_id=1, source_target_pairs={{1,0},{2,1},{3,2},{0,3},{5,4},{6,5},{7,6},{4,7},{9,8},{10,9},{11,1... | collective-permute-start | bytes 442376 | tf_op jit(solution)/shard_map/ppermute | solution.py:173
  64.1 0.8 fusion.2.term_ref
  64.9 3.6 %collective-permute-done.4 = bf16[12,12,2,256]{3,2,1,0:T(2,128)(2,1)S(1)} collective-permute-done((bf16[12,12,2,256]{3,2,1,0:T(2,128)(2,1)S(1)}, bf16[12,12,2,256]{3,2,1,0:T(2,128)(2,1)S(1)}, u32[]{:S(2)}, u32[]{:S(2)}) %collective-permute-start.4) | collective-permute-done | bytes 147488 | tf_op jit(solution)/shard_map/ppermute | solution.py:172
  68.5 1.0 collective-permute-done.5
  69.4 2.1 %maximum_convert_fusion.padded_ref = f32[12,12,12,256]{3,2,1,0:T(8,128)} fusion(bf16[12,12,2,256]{3,2,1,0:T(2,128)(2,1)S(1)} %collective-permute-done.5, bf16[12,2,8,256]{3,2,1,0:T(8,128)(2,1)S(1)} %collective-permute-done.3, bf16[4,8,8,256]{3,2,1,0:T(8,128)(2,1)S(1)} %add_convert_fusion, bf16[4,8,8,256]{3,2,1,0:T(8,128)(2,1)S(1)} %bitcast.24, ...), kind=kLoop, calls=%fused_computation | loop fusion | flops 6193152 | bytes 2654208 | tf_op jit(solution)/shard_map/convert_element_type | solution.py:211
  71.5 28.3 %shard_map.105 = bf16[512,256]{1,0:T(8,128)(2,1)} custom-call(f32[12,12,12,256]{3,2,1,0:T(8,128)} %maximum_convert_fusion.padded_ref, s32[512,98]{1,0:T(8,128)} %bitcast.29, f32[256,98]{1,0:T(8,128)} %bitcast.28, f32[98,256]{1,0:T(8,128)} %cols_ref.1, bf16[256,256]{1,0:T(8,128)(2,1)} %base_ref.1, f32[1,256]{1,0:T(1,128)} %fusion.2.term_ref), custom_call_target="tpu_custom_call" | custom-call | tf_op jit(solution)/shard_map/pallas_call | solution.py:213
  99.8 0.9 fusion.1
  100.6 1.4 %collective-permute-start.6 = (bf16[2,8,8,256]{3,2,1,0:T(8,128)(2,1)S(1)}, bf16[2,8,8,256]{3,2,1,0:T(8,128)(2,1)S(1)}, u32[]{:S(2)}, u32[]{:S(2)}) collective-permute-start(bf16[2,8,8,256]{3,2,1,0:T(8,128)(2,1)S(1)} %bitcast.33), channel_id=1, source_target_pairs={{0,16},{16,0},{1,17},{17,1},{2,18},{18,2},{3,19},{19,3},{4,20},{20... | collective-permute-start | bytes 196616 | tf_op jit(solution)/shard_map/ppermute | solution.py:172
  102.1 0.7 collective-permute-start.7
  102.7 2.2 %collective-permute-done.6 = bf16[2,8,8,256]{3,2,1,0:T(8,128)(2,1)S(1)} collective-permute-done((bf16[2,8,8,256]{3,2,1,0:T(8,128)(2,1)S(1)}, bf16[2,8,8,256]{3,2,1,0:T(8,128)(2,1)S(1)}, u32[]{:S(2)}, u32[]{:S(2)}) %collective-permute-start.6) | collective-permute-done | bytes 65568 | tf_op jit(solution)/shard_map/ppermute | solution.py:172
  105.0 1.3 %collective-permute-done.7 = bf16[2,8,8,256]{3,2,1,0:T(8,128)(2,1)S(1)} collective-permute-done((bf16[2,8,8,256]{3,2,1,0:T(8,128)(2,1)S(1)}, bf16[2,8,8,256]{3,2,1,0:T(8,128)(2,1)S(1)}, u32[]{:S(2)}, u32[]{:S(2)}) %collective-permute-start.7) | collective-permute-done | bytes 65568 | tf_op jit(solution)/shard_map/ppermute | solution.py:173
  106.3 1.7 %pad_maximum_fusion = bf16[12,8,8,256]{3,2,1,0:T(8,128)(2,1)} fusion(bf16[2,8,8,256]{3,2,1,0:T(8,128)(2,1)S(1)} %collective-permute-done.7, bf16[8,8,8,256]{3,2,1,0:T(8,128)(2,1)} %bitcast.25, bf16[2,8,8,256]{3,2,1,0:T(8,128)(2,1)S(1)} %collective-permute-done.6), kind=kLoop, calls=%fused_computation.1 | loop fusion | flops 393216 | bytes 786432 | tf_op jit(solution)/shard_map/concatenate | solution.py:174
  108.1 5.6 %shard_map.106 = f32[1,4096]{1,0:T(1,128)} custom-call(bf16[768,256]{1,0:T(8,128)(2,1)} %bitcast.27, bf16[4096,256]{1,0:T(8,128)(2,1)} %mult_ref.3, s32[1,4096]{1,0:T(1,128)} %bitcast.31), custom_call_target="tpu_custom_call" | custom-call | tf_op jit(solution)/shard_map/pallas_call | solution.py:230
  (15 shorter events, 0.3 us)
Async XLA Ops:
  0.6 63.5 %copy-start = (f32[256,256]{1,0:T(8,128)S(1)}, f32[256,256]{1,0:T(8,128)}, u32[]{:S(2)}) copy-start(f32[256,256]{1,0:T(8,128)} %param.17) | copy-start | bytes 786436
  6.2 12.3 %copy-start.1 = (f32[98,256]{1,0:T(8,128)S(1)}, f32[98,256]{1,0:T(8,128)}, u32[]{:S(2)}) copy-start(f32[98,256]{1,0:T(8,128)} %param.14) | copy-start | bytes 301060
  6.2 13.1 %copy-start.2 = (f32[1,256]{1,0:T(1,128)S(1)}, f32[1,256]{1,0:T(1,128)}, u32[]{:S(2)}) copy-start(f32[1,256]{1,0:T(1,128)} %get-tuple-element.5) | copy-start | bytes 3076
  7.4 7.3 %collective-permute-start = (bf16[4,8,8,256]{3,2,1,0:T(8,128)(2,1)S(1)}, bf16[4,8,8,256]{3,2,1,0:T(8,128)(2,1)S(1)}, u32[]{:S(2)}, u32[]{:S(2)}) collective-permute-start(bf16[4,8,8,256]{3,2,1,0:T(8,128)(2,1)S(1)} %convert_element_type.16), channel_id=1, source_target_pairs={{0,16},{16,0},{1,17},{17,1},{2,18},{18,2},{3,19},{19,3},{4,20},{20... | collective-permute-start | bytes 393224 | tf_op jit(solution)/shard_map/ppermute | solution.py:201
  10.4 6.3 %collective-permute-start.1 = (bf16[4,8,8,256]{3,2,1,0:T(8,128)(2,1)S(1)}, bf16[4,8,8,256]{3,2,1,0:T(8,128)(2,1)S(1)}, u32[]{:S(2)}, u32[]{:S(2)}) collective-permute-start(bf16[4,8,8,256]{3,2,1,0:T(8,128)(2,1)S(1)} %convert_element_type.18), channel_id=1, source_target_pairs={{16,0},{0,16},{17,1},{1,17},{18,2},{2,18},{19,3},{3,19},{20,4},{4,... | collective-permute-start | bytes 393224 | tf_op jit(solution)/shard_map/ppermute | solution.py:202
  16.7 43.3 %collective-permute-start.2 = (bf16[12,2,8,256]{3,2,1,0:T(8,128)(2,1)S(1)}, bf16[12,2,8,256]{3,2,1,0:T(8,128)(2,1)S(1)}, u32[]{:S(2)}, u32[]{:S(2)}) collective-permute-start(bf16[12,2,8,256]{3,2,1,0:T(8,128)(2,1)S(1)} %get-tuple-element.10), channel_id=1, source_target_pairs={{0,4},{4,8},{8,12},{12,0},{1,5},{5,9},{9,13},{13,1},{2,6},{6,10},{... | collective-permute-start | bytes 294920 | tf_op jit(solution)/shard_map/ppermute | solution.py:172
  16.8 43.2 %collective-permute-start.3 = (bf16[12,2,8,256]{3,2,1,0:T(8,128)(2,1)S(1)}, bf16[12,2,8,256]{3,2,1,0:T(8,128)(2,1)S(1)}, u32[]{:S(2)}, u32[]{:S(2)}) collective-permute-start(bf16[12,2,8,256]{3,2,1,0:T(8,128)(2,1)S(1)} %get-tuple-element.11), channel_id=1, source_target_pairs={{4,0},{8,4},{12,8},{0,12},{5,1},{9,5},{13,9},{1,13},{6,2},{10,6},{... | collective-permute-start | bytes 294920 | tf_op jit(solution)/shard_map/ppermute | solution.py:173
  60.2 8.3 %collective-permute-start.4 = (bf16[12,12,2,256]{3,2,1,0:T(2,128)(2,1)S(1)}, bf16[12,12,2,256]{3,2,1,0:T(2,128)(2,1)S(1)}, u32[]{:S(2)}, u32[]{:S(2)}) collective-permute-start(bf16[12,12,2,256]{3,2,1,0:T(2,128)(2,1)S(1)} %get-tuple-element.8), channel_id=1, source_target_pairs={{0,1},{1,2},{2,3},{3,0},{4,5},{5,6},{6,7},{7,4},{8,9},{9,10},{10,1... | collective-permute-start | bytes 442376 | tf_op jit(solution)/shard_map/ppermute | solution.py:172
  61.8 7.7 %collective-permute-start.5 = (bf16[12,12,2,256]{3,2,1,0:T(2,128)(2,1)S(1)}, bf16[12,12,2,256]{3,2,1,0:T(2,128)(2,1)S(1)}, u32[]{:S(2)}, u32[]{:S(2)}) collective-permute-start(bf16[12,12,2,256]{3,2,1,0:T(2,128)(2,1)S(1)} %get-tuple-element.9), channel_id=1, source_target_pairs={{1,0},{2,1},{3,2},{0,3},{5,4},{6,5},{7,6},{4,7},{9,8},{10,9},{11,1... | collective-permute-start | bytes 442376 | tf_op jit(solution)/shard_map/ppermute | solution.py:173
  100.6 4.3 %collective-permute-start.6 = (bf16[2,8,8,256]{3,2,1,0:T(8,128)(2,1)S(1)}, bf16[2,8,8,256]{3,2,1,0:T(8,128)(2,1)S(1)}, u32[]{:S(2)}, u32[]{:S(2)}) collective-permute-start(bf16[2,8,8,256]{3,2,1,0:T(8,128)(2,1)S(1)} %bitcast.33), channel_id=1, source_target_pairs={{0,16},{16,0},{1,17},{17,1},{2,18},{18,2},{3,19},{19,3},{4,20},{20... | collective-permute-start | bytes 196616 | tf_op jit(solution)/shard_map/ppermute | solution.py:172
  102.1 4.3 %collective-permute-start.7 = (bf16[2,8,8,256]{3,2,1,0:T(8,128)(2,1)S(1)}, bf16[2,8,8,256]{3,2,1,0:T(8,128)(2,1)S(1)}, u32[]{:S(2)}, u32[]{:S(2)}) collective-permute-start(bf16[2,8,8,256]{3,2,1,0:T(8,128)(2,1)S(1)} %bitcast.32), channel_id=1, source_target_pairs={{16,0},{0,16},{17,1},{1,17},{18,2},{2,18},{19,3},{3,19},{20,4},{4,... | collective-permute-start | bytes 196616 | tf_op jit(solution)/shard_map/ppermute | solution.py:173
where the time goes:
time: 114 us
  blocking collectives  40.8 us (36%)
  Pallas kernels  39.4 us (35%)
  waiting for transfers between devices  13.3 us (12%)
  starting transfers between devices  10.9 us (10%)
  other arithmetic  4.1 us (4%)
  local copies, waits for them, and re-layouts  3.7 us (3%)
    psum x1, blocking collectives, per_device(): cell = lax.psum(cell_part, ('rows', 'bx', 'by'))  40.8 us
    pallas_call x1, Pallas kernels, per_device(): pl.pallas_call(functools.partial(field_kernel, (depth, width_x, width_y))...  28.3 us
    ppermute x3, waiting for transfers between devices, padded_2(): lax.ppermute(lax.slice_in_dim(x, length - 2, length, axis=dim), axis, up)  5.82 us
    pallas_call x1, Pallas kernels, per_device(): pl.pallas_call(moments_kernel, out_shape=(jax.ShapeDtypeStruct((near, com...  5.58 us
    pallas_call x1, Pallas kernels, per_device(): pl.pallas_call(pairs_kernel, out_shape=jax.ShapeDtypeStruct((1, pairs), j...  5.56 us
    ppermute x3, starting transfers between devices, padded_2(): after = lax.ppermute(lax.slice_in_dim(x, 0, 2, axis=dim), axis, down)  4.73 us
    ppermute x1, waiting for transfers between devices, per_device(): low = lax.ppermute(partial[depth:].astype(jnp.bfloat16), 'rows', up)  3.26 us
    ppermute x3, starting transfers between devices, padded_2(): lax.ppermute(lax.slice_in_dim(x, length - 2, length, axis=dim), axis, up)  3.03 us
  transfers between devices with their start and end apart: 8, of which 6 were waited for; matrix products, arithmetic and copies ran while one was open for 2% of the time, Pallas kernels for 0%

commit v1 on v0

--- a/solution.py
+++ b/solution.py
@@ -21,7 +21,7 @@
     return listed
 
 
-def moments_kernel(mult_ref, dens_ref, live_ref, box_ref, near_ref, cell_ref):
+def add_moments(mult_ref, dens_ref, live_ref, box_ref, near_ref):
     near = near_ref.shape[0]
     labels = lax.broadcasted_iota(jnp.int32, (near, PAIR_CHUNK), 0)
     near_ref[...] = jnp.zeros_like(near_ref)
@@ -34,12 +34,11 @@
         return carry
 
     lax.fori_loop(0, mult_ref.shape[0] // PAIR_CHUNK, step, 0)
-    cell_ref[...] = jnp.sum(near_ref[...], 0, keepdims=True)
-
-
-def pairs_kernel(locals_ref, mult_ref, box_ref, out_ref):
-    near = locals_ref.shape[0]
-    labels = lax.broadcasted_iota(jnp.int32, (near, PAIR_CHUNK), 0)
+
+
+def add_pairs(locals_ref, first, mult_ref, box_ref, pairs_ref, fresh):
+    count = locals_ref.shape[0]
+    labels = lax.broadcasted_iota(jnp.int32, (count, PAIR_CHUNK), 0) + first
 
     def step(index, carry):
         at = pl.ds(pl.multiple_of(index * PAIR_CHUNK, PAIR_CHUNK), PAIR_CHUNK)
@@ -50,10 +49,212 @@
             preferred_element_type=jnp.float32,
         )
         hits = jnp.where(labels == box_ref[:, at], values, 0.0)
-        out_ref[:, at] = jnp.sum(hits, 0, keepdims=True)
+        found = jnp.sum(hits, 0, keepdims=True)
+        pairs_ref[:, at] = found if fresh else pairs_ref[:, at] + found
         return carry
 
     lax.fori_loop(0, mult_ref.shape[0] // PAIR_CHUNK, step, 0)
+
+
+def neighbour(axis, move):
+    count = lax.axis_size(axis)
+    return {axis: lax.rem(lax.axis_index(axis) + (move + count), count)}
+
+
+def send(source, target, sems, index, device):
+    copy = pltpu.make_async_remote_copy(
+        src_ref=source,
+        dst_ref=target,
+        send_sem=sems.at[0, index],
+        recv_sem=sems.at[1, index],
+        device_id=device,
+        device_id_type=pl.DeviceIdType.MESH,
+    )
+    copy.start()
+    return copy
+
+
+def share_cells(axis, own_ref, slots_ref, sems):
+    return [
+        send(own_ref, slots_ref.at[move - 1], sems, move - 1, neighbour(axis, move))
+        for move in range(1, lax.axis_size(axis))
+    ]
+
+
+def collect_cells(copies, own_ref, slots_ref):
+    value = own_ref[...]
+    for place, copy in enumerate(copies):
+        copy.wait_recv()
+        value = value + slots_ref[place]
+    return value
+
+
+def fused_kernel(
+    sizes, mult_ref, dens_ref, live_ref, box_ref, mask_ref, rows_ref, cols_ref, base_ref, lattice_ref,
+    out_ref, pairs_ref,
+    near_ref, zsend_ref, zrecv_ref, full_ref, padded_ref, pack_ref, ysend_ref, yrecv_ref, lrecv_ref,
+    cells_ref, cells_r, cells_x, cells_y, gates_ref, wide_ref, shifted_ref, left_ref, total_ref,
+    zsem, xsem, ysem, lsem, crsem, cxsem, cysem,
+):
+    size_z, size_x, size_y = sizes
+    plane = size_x * size_y
+    near_z, near_x = size_z + 4, size_x + 4
+    comps = near_ref.shape[1]
+    axes = ("rows", "bx", "by")
+    barrier = pltpu.get_barrier_semaphore()
+    peers = 0
+    for axis in axes:
+        for move in range(1, lax.axis_size(axis)):
+            pl.semaphore_signal(
+                barrier, inc=1, device_id=neighbour(axis, move), device_id_type=pl.DeviceIdType.MESH
+            )
+            peers += 1
+
+    add_moments(mult_ref, dens_ref, live_ref, box_ref, near_ref)
+    zsend_ref[0] = near_ref[: 4 * plane].astype(jnp.bfloat16)
+    zsend_ref[1] = near_ref[size_z * plane :].astype(jnp.bfloat16)
+    pl.semaphore_wait(barrier, peers)
+    waits = [
+        send(zsend_ref.at[0], zrecv_ref.at[1], zsem, 0, neighbour("rows", -1)),
+        send(zsend_ref.at[1], zrecv_ref.at[0], zsem, 1, neighbour("rows", 1)),
+    ]
+    zcopies = list(waits)
+    cells_ref[0] = jnp.broadcast_to(jnp.sum(near_ref[...], 0, keepdims=True), (8, comps))
+    rcopies = share_cells("rows", cells_ref.at[0], cells_r, crsem)
+    waits += rcopies
+
+    expand_operators(rows_ref, cols_ref, base_ref, wide_ref)
+
+    for copy in zcopies:
+        copy.wait_recv()
+    near_ref[: 4 * plane] += zrecv_ref[0].astype(jnp.float32)
+    near_ref[size_z * plane :] += zrecv_ref[1].astype(jnp.float32)
+    own = pl.ds(2 * size_y, plane)
+    for level in range(near_z):
+        full_ref[level, own, :] = near_ref[level * plane : (level + 1) * plane].astype(jnp.bfloat16)
+    edge = 2 * size_y
+    xcopies = [
+        send(
+            full_ref.at[:, pl.ds(edge, edge), :], full_ref.at[:, pl.ds(edge + plane, edge), :],
+            xsem, 0, neighbour("bx", -1),
+        ),
+        send(
+            full_ref.at[:, pl.ds(plane, edge), :], full_ref.at[:, pl.ds(0, edge), :],
+            xsem, 1, neighbour("bx", 1),
+        ),
+    ]
+    waits += xcopies
+    cells_ref[1] = collect_cells(rcopies, cells_ref.at[0], cells_r)
+    bcopies = share_cells("bx", cells_ref.at[1], cells_x, cxsem)
+    waits += bcopies
+
+    expand_masks(mask_ref, gates_ref)
+
+    for copy in xcopies:
+        copy.wait_recv()
+
+    def pack(level, carry):
+        values = full_ref[level].astype(jnp.float32).reshape(near_x, size_y, comps)
+        padded_ref[level, :, 2 : 2 + size_y, :] = values
+        for x in range(near_x):
+            pack_ref[0, level, 2 * x : 2 * x + 2, :] = values[x, :2, :]
+            pack_ref[1, level, 2 * x : 2 * x + 2, :] = values[x, size_y - 2 :, :]
+        return carry
+
+    lax.fori_loop(0, near_z, pack, 0)
+    ysend_ref[...] = pack_ref[...].reshape(ysend_ref.shape).astype(jnp.bfloat16)
+    ycopies = [
+        send(ysend_ref.at[0], yrecv_ref.at[1], ysem, 0, neighbour("by", -1)),
+        send(ysend_ref.at[1], yrecv_ref.at[0], ysem, 1, neighbour("by", 1)),
+    ]
+    waits += ycopies
+    cells_ref[2] = collect_cells(bcopies, cells_ref.at[1], cells_x)
+    ccopies = share_cells("by", cells_ref.at[2], cells_y, cysem)
+    waits += ccopies
+    for copy in ycopies:
+        copy.wait_recv()
+    pack_ref[...] = yrecv_ref[...].astype(jnp.float32).reshape(pack_ref.shape)
+
+    def unpack(level, carry):
+        for x in range(near_x):
+            padded_ref[level, x, :2, :] = pack_ref[0, level, 2 * x : 2 * x + 2, :]
+            padded_ref[level, x, 2 + size_y :, :] = pack_ref[1, level, 2 * x : 2 * x + 2, :]
+        return carry
+
+    lax.fori_loop(0, near_z, unpack, 0)
+    shifted_copies(padded_ref, shifted_ref)
+
+    cell = collect_cells(ccopies, cells_ref.at[2], cells_y)
+    term = jnp.dot(
+        cell, lattice_ref[...], precision=lax.Precision.HIGHEST, preferred_element_type=jnp.float32
+    )
+    total_ref[...] = jnp.broadcast_to(term[:1], total_ref.shape)
+    far_field(shifted_ref, gates_ref, wide_ref, total_ref, left_ref, sizes)
+    out_ref[...] = total_ref[...].astype(jnp.bfloat16)
+    boxes = size_z * plane
+    lcopies = [
+        send(out_ref.at[pl.ds(0, 2 * plane)], lrecv_ref.at[1], lsem, 0, neighbour("rows", -1)),
+        send(out_ref.at[pl.ds(boxes - 2 * plane, 2 * plane)], lrecv_ref.at[0], lsem, 1, neighbour("rows", 1)),
+    ]
+    waits += lcopies
+    add_pairs(out_ref, 2 * plane, mult_ref, box_ref, pairs_ref, True)
+    for copy in lcopies:
+        copy.wait_recv()
+    add_pairs(lrecv_ref.at[0], 0, mult_ref, box_ref, pairs_ref, False)
+    add_pairs(lrecv_ref.at[1], boxes + 2 * plane, mult_ref, box_ref, pairs_ref, False)
+    for copy in waits:
+        copy.wait_send()
+
+
+def per_device(
+    pair_mult, pair_dens, pair_live, pair_box, inter_mask, row_scale, col_scale, base, lattice
+):
+    pairs, comps = pair_mult.shape
+    depth, width_x, width_y, offsets = inter_mask.shape
+    plane = width_x * width_y
+    boxes = depth * plane
+    near = boxes + 4 * plane
+    edge_rows = (depth + 4) * (width_x + 4) * 2
+    counts = [lax.axis_size(axis) - 1 for axis in ("rows", "bx", "by")]
+    b16, f32 = jnp.bfloat16, jnp.float32
+    box_locals, pair_j = pl.pallas_call(
+        functools.partial(fused_kernel, (depth, width_x, width_y)),
+        out_shape=(
+            jax.ShapeDtypeStruct((boxes, comps), b16),
+            jax.ShapeDtypeStruct((1, pairs), f32),
+        ),
+        in_specs=[VMEM] * 9,
+        out_specs=(VMEM, VMEM),
+        scratch_shapes=[
+            pltpu.VMEM((near, comps), f32),
+            pltpu.VMEM((2, 4 * plane, comps), b16),
+            pltpu.VMEM((2, 4 * plane, comps), b16),
+            pltpu.VMEM((depth + 4, (width_x + 4) * width_y, comps), b16),
+            pltpu.VMEM((depth + 4, width_x + 4, width_y + 4, comps), f32),
+            pltpu.VMEM((2, depth + 4, 2 * (width_x + 4), comps), f32),
+            pltpu.VMEM((2, edge_rows, comps), b16),
+            pltpu.VMEM((2, edge_rows, comps), b16),
+            pltpu.VMEM((2, 2 * plane, comps), b16),
+            pltpu.VMEM((3, 8, comps), f32),
+        ]
+        + [pltpu.VMEM((count, 8, comps), f32) for count in counts]
+        + [
+            pltpu.VMEM((offsets, boxes, 128), b16),
+            pltpu.VMEM((offsets, comps, comps), b16),
+            pltpu.VMEM((5, 2, depth + 4, (width_x + 4) * width_y, comps), b16),
+            pltpu.VMEM((boxes, 5 * comps), b16),
+            pltpu.VMEM((boxes, comps), f32),
+        ]
+        + [pltpu.SemaphoreType.DMA((2, 2))] * 4
+        + [pltpu.SemaphoreType.DMA((2, count)) for count in counts],
+        compiler_params=pltpu.CompilerParams(
+            vmem_limit_bytes=56 * 1024 * 1024, collective_id=0, has_side_effects=True
+        ),
+    )(
+        pair_mult, pair_dens.reshape(1, pairs), pair_live.reshape(1, pairs), pair_box.reshape(1, pairs),
+        inter_mask.reshape(boxes, offsets), row_scale.T, col_scale, base, lattice,
+    )
+    return (box_locals.reshape(depth, width_x, width_y, comps), pair_j.reshape(pairs))
 
 
 def expand_operators(rows_ref, cols_ref, base_ref, wide_ref):
@@ -148,95 +349,6 @@
     lax.fori_loop(0, 9, inner, 0)
 
 
-def field_kernel(
-    sizes, padded_ref, mask_ref, rows_ref, cols_ref, base_ref, term_ref, out_ref,
-    gates_ref, wide_ref, shifted_ref, left_ref, total_ref,
-):
-    expand_operators(rows_ref, cols_ref, base_ref, wide_ref)
-    expand_masks(mask_ref, gates_ref)
-    shifted_copies(padded_ref, shifted_ref)
-    total_ref[...] = jnp.broadcast_to(term_ref[...], total_ref.shape)
-    far_field(shifted_ref, gates_ref, wide_ref, total_ref, left_ref, sizes)
-    out_ref[...] = total_ref[...].astype(jnp.bfloat16)
-
-
-def ring(axis):
-    count = lax.axis_size(axis)
-    up = [(i, (i + 1) % count) for i in range(count)]
-    return up, [(j, i) for i, j in up]
-
-
-def padded_2(x, axis, dim):
-    up, down = ring(axis)
-    length = x.shape[dim]
-    before = lax.ppermute(lax.slice_in_dim(x, length - 2, length, axis=dim), axis, up)
-    after = lax.ppermute(lax.slice_in_dim(x, 0, 2, axis=dim), axis, down)
-    return jnp.concatenate([before, x, after], axis=dim)
-
-
-def per_device(
-    pair_mult, pair_dens, pair_live, pair_box, inter_mask, row_scale, col_scale, base, lattice
-):
-    pairs, comps = pair_mult.shape
-    depth, width_x, width_y, offsets = inter_mask.shape
-    boxes = depth * width_x * width_y
-    near = (depth + 4) * width_x * width_y
-    box_row = pair_box.reshape(1, pairs)
-    params = pltpu.CompilerParams(vmem_limit_bytes=56 * 1024 * 1024)
-    partial, cell_part = pl.pallas_call(
-        moments_kernel,
-        out_shape=(
-            jax.ShapeDtypeStruct((near, comps), jnp.float32),
-            jax.ShapeDtypeStruct((1, comps), jnp.float32),
-        ),
-        in_specs=[VMEM] * 4,
-        out_specs=(VMEM, VMEM),
-        compiler_params=params,
-    )(pair_mult, pair_dens.reshape(1, pairs), pair_live.reshape(1, pairs), box_row)
-    cell = lax.psum(cell_part, ("rows", "bx", "by"))
-    term = jnp.dot(cell, lattice, precision=lax.Precision.HIGHEST)
-
-    partial = partial.reshape(depth + 4, width_x, width_y, comps)
-    up, down = ring("rows")
-    low = lax.ppermute(partial[depth:].astype(jnp.bfloat16), "rows", up)
-    high = lax.ppermute(partial[:4].astype(jnp.bfloat16), "rows", down)
-    full = jnp.concatenate(
-        [
-            partial[:4] + low.astype(jnp.float32),
-            partial[4:depth],
-            partial[depth:] + high.astype(jnp.float32),
-        ],
-        axis=0,
-    ).astype(jnp.bfloat16)
-    padded = padded_2(padded_2(full, "bx", 1), "by", 2).astype(jnp.float32)
-
-    box_locals = pl.pallas_call(
-        functools.partial(field_kernel, (depth, width_x, width_y)),
-        out_shape=jax.ShapeDtypeStruct((boxes, comps), jnp.bfloat16),
-        in_specs=[VMEM] * 6,
-        out_specs=VMEM,
-        scratch_shapes=[
-            pltpu.VMEM((offsets, boxes, 128), jnp.bfloat16),
-            pltpu.VMEM((offsets, comps, comps), jnp.bfloat16),
-            pltpu.VMEM((5, 2, depth + 4, (width_x + 4) * width_y, comps), jnp.bfloat16),
-            pltpu.VMEM((boxes, 5 * comps), jnp.bfloat16),
-            pltpu.VMEM((boxes, comps), jnp.float32),
-        ],
-        compiler_params=params,
-    )(padded, inter_mask.reshape(boxes, offsets), row_scale.T, col_scale, base, term)
-
-    box_locals = box_locals.reshape(depth, width_x, width_y, comps)
-    near_locals = padded_2(box_locals, "rows", 0).reshape(near, comps)
-    pair_j = pl.pallas_call(
-        pairs_kernel,
-        out_shape=jax.ShapeDtypeStruct((1, pairs), jnp.float32),
-        in_specs=[VMEM] * 3,
-        out_specs=VMEM,
-        compiler_params=params,
-    )(near_locals, pair_mult, box_row)
-    return (box_locals, pair_j.reshape(pairs))
-
-
 def solution(mesh):
     return jax.shard_map(
         per_device,

time: 114 us -> 58.9 us (0.52)
  blocking collectives: 40.8 us -> 0 us
  Pallas kernels: 39.4 us -> 53.4 us
  waiting for transfers between devices: 13.3 us -> 0 us
  starting transfers between devices: 10.9 us -> 0 us
  other arithmetic: 4.1 us -> 0 us
    psum x1 -> x0, blocking collectives: 40.8 us -> none  [per_device(): cell = lax.psum(cell_part, ('rows', 'bx', 'by'))]
    pallas_call x3 -> x1, Pallas kernels: 39.4 us -> 53.4 us  [per_device(): pl.pallas_call(functools.partial(fused_kernel, (depth, width_x, width_y))...]
    ppermute x8 -> x0, waiting for transfers between devices: 13.3 us -> none  [the longest x3 5.82 us: padded_2(): lax.ppermute(lax.slice_in_dim(x, length - 2, length, axis=dim), axis, up)]
    ppermute x8 -> x0, starting transfers between devices: 10.9 us -> none  [the longest x3 4.73 us: padded_2(): after = lax.ppermute(lax.slice_in_dim(x, 0, 2, axis=dim), axis, down)]
    unnamed x7 -> x3, local copies, waits for them, and re-layouts: 0.76 us -> 4.65 us
    slice x3 -> x0, local copies, waits for them, and re-layouts: 2.94 us -> none  [the longest x1 1.1 us: per_device(): partial[:4] + low.astype(jnp.float32)]
    convert_element_type x3 -> x0, other arithmetic: 2.08 us -> none  [the longest x1 2.05 us: per_device(): padded = padded_2(padded_2(full, 'bx', 1), 'by', 2).astype(jnp.float32)]
    concatenate x1 -> x0, other arithmetic: 1.74 us -> none  [padded_2(): return jnp.concatenate([before, x, after], axis=dim)]
  transfers between devices with their start and end apart: 8 -> 0, of which waited for: 6 -> 0; matrix products, arithmetic and copies ran while one was open for 2% -> 0% of each run, Pallas kernels for 0% -> 0%
where the time goes in v1:
time: 58.9 us; the launch traced here: 58.7 us
  Pallas kernels  53.4 us (91%)
  local copies, waits for them, and re-layouts  4.65 us (8%)
  between operations  0.64 us (1%)
    pallas_call x1, Pallas kernels, per_device(): pl.pallas_call(functools.partial(fused_kernel, (depth, width_x, width_y))...  53.4 us
    unnamed x3, local copies, waits for them, and re-layouts  4.65 us

profile of v1, /device:TPU:0, one launch (start us, length us, event | category | flops | bytes accessed | tf_op | source)
XLA Modules:
  0.0 58.7 jit_solution(14503134238458287265)
XLA Ops:
  0.6 1.7 %copy.11 = f32[98,256]{0,1:T(8,128)} copy(f32[98,256]{1,0:T(8,128)} %param.14) | data formatting | bytes 200704 | tf_op args[5]
  2.3 53.4 %shard_map.104 = (bf16[512,256]{1,0:T(8,128)(2,1)}, f32[1,4096]{1,0:T(1,128)}) custom-call(bf16[4096,256]{1,0:T(8,128)(2,1)} %mult_ref.1, f32[1,4096]{1,0:T(1,128)} %bitcast.10, s32[1,4096]{1,0:T(1,128)} %bitcast.11, s32[1,4096]{1,0:T(1,128)} %bitcast.12, s32[512,98]{1,0:T(8,128)} %bitcast.8, f32[256,98]{1,0:T(8,128)} %bitcast.7, f32[98,256]{1,0:T(8,128)} %cols_ref.1, ...), custom_call_target="tpu_custom_call" | custom-call | tf_op jit(solution)/shard_map/pallas_call | solution.py:220
  55.7 1.7 %copy.14 = bf16[8,8,8,256]{3,2,1,0:T(8,128)(2,1)} copy(bf16[8,8,8,256]{3,2,1,0:T(8,128)(2,1)} %bitcast.9) | data formatting | bytes 524288
  57.4 1.3 %copy.15 = f32[4096]{0:T(1024)} copy(f32[4096]{0:T(1024)} %bitcast.13) | data formatting | bytes 32768

commit v2 on v1

--- a/solution.py
+++ b/solution.py
@@ -7,7 +7,7 @@
 from jax.experimental.pallas import tpu as pltpu
 from jax.sharding import PartitionSpec as P
 
-PAIR_CHUNK = 512
+PAIR_CHUNK = 1024
 VMEM = pl.BlockSpec(memory_space=pltpu.VMEM)
 
 
@@ -36,9 +36,11 @@
     lax.fori_loop(0, mult_ref.shape[0] // PAIR_CHUNK, step, 0)
 
 
-def add_pairs(locals_ref, first, mult_ref, box_ref, pairs_ref, fresh):
+def add_pairs(locals_ref, first, jump, mult_ref, box_ref, pairs_ref, fresh):
     count = locals_ref.shape[0]
     labels = lax.broadcasted_iota(jnp.int32, (count, PAIR_CHUNK), 0) + first
+    if jump:
+        labels = labels + jnp.where(labels >= count // 2, jump, 0)
 
     def step(index, carry):
         at = pl.ds(pl.multiple_of(index * PAIR_CHUNK, PAIR_CHUNK), PAIR_CHUNK)
@@ -93,7 +95,7 @@
     sizes, mult_ref, dens_ref, live_ref, box_ref, mask_ref, rows_ref, cols_ref, base_ref, lattice_ref,
     out_ref, pairs_ref,
     near_ref, zsend_ref, zrecv_ref, full_ref, padded_ref, pack_ref, ysend_ref, yrecv_ref, lrecv_ref,
-    cells_ref, cells_r, cells_x, cells_y, gates_ref, wide_ref, shifted_ref, left_ref, total_ref,
+    cells_ref, cells_r, cells_x, cells_y, gates_ref, wide_ref, shifted_ref, total_ref, rows_pad, turned_ref,
     zsem, xsem, ysem, lsem, crsem, cxsem, cysem,
 ):
     size_z, size_x, size_y = sizes
@@ -123,7 +125,11 @@
     rcopies = share_cells("rows", cells_ref.at[0], cells_r, crsem)
     waits += rcopies
 
-    expand_operators(rows_ref, cols_ref, base_ref, wide_ref)
+    rows_pad[...] = jnp.zeros_like(rows_pad)
+    rows_pad[: rows_ref.shape[0], :] = rows_ref[...]
+    turned_ref[...] = rows_pad[...].T
+    expand_operators(turned_ref, cols_ref, base_ref, wide_ref)
+    expand_masks(mask_ref, gates_ref, 0, 1)
 
     for copy in zcopies:
         copy.wait_recv()
@@ -148,7 +154,7 @@
     bcopies = share_cells("bx", cells_ref.at[1], cells_x, cxsem)
     waits += bcopies
 
-    expand_masks(mask_ref, gates_ref)
+    expand_masks(mask_ref, gates_ref, 1, 2)
 
     for copy in xcopies:
         copy.wait_recv()
@@ -171,6 +177,8 @@
     cells_ref[2] = collect_cells(bcopies, cells_ref.at[1], cells_x)
     ccopies = share_cells("by", cells_ref.at[2], cells_y, cysem)
     waits += ccopies
+    shifted_copies(padded_ref, shifted_ref, (2,))
+    expand_masks(mask_ref, gates_ref, 2, 4)
     for copy in ycopies:
         copy.wait_recv()
     pack_ref[...] = yrecv_ref[...].astype(jnp.float32).reshape(pack_ref.shape)
@@ -182,26 +190,25 @@
         return carry
 
     lax.fori_loop(0, near_z, unpack, 0)
-    shifted_copies(padded_ref, shifted_ref)
+    shifted_copies(padded_ref, shifted_ref, (0, 1, 3, 4))
 
     cell = collect_cells(ccopies, cells_ref.at[2], cells_y)
     term = jnp.dot(
         cell, lattice_ref[...], precision=lax.Precision.HIGHEST, preferred_element_type=jnp.float32
     )
     total_ref[...] = jnp.broadcast_to(term[:1], total_ref.shape)
-    far_field(shifted_ref, gates_ref, wide_ref, total_ref, left_ref, sizes)
+    far_field(shifted_ref, gates_ref, wide_ref, total_ref, sizes)
     out_ref[...] = total_ref[...].astype(jnp.bfloat16)
     boxes = size_z * plane
     lcopies = [
-        send(out_ref.at[pl.ds(0, 2 * plane)], lrecv_ref.at[1], lsem, 0, neighbour("rows", -1)),
-        send(out_ref.at[pl.ds(boxes - 2 * plane, 2 * plane)], lrecv_ref.at[0], lsem, 1, neighbour("rows", 1)),
+        send(out_ref.at[pl.ds(0, 2 * plane)], lrecv_ref.at[pl.ds(2 * plane, 2 * plane)], lsem, 0, neighbour("rows", -1)),
+        send(out_ref.at[pl.ds(boxes - 2 * plane, 2 * plane)], lrecv_ref.at[pl.ds(0, 2 * plane)], lsem, 1, neighbour("rows", 1)),
     ]
     waits += lcopies
-    add_pairs(out_ref, 2 * plane, mult_ref, box_ref, pairs_ref, True)
+    add_pairs(out_ref, 2 * plane, 0, mult_ref, box_ref, pairs_ref, True)
     for copy in lcopies:
         copy.wait_recv()
-    add_pairs(lrecv_ref.at[0], 0, mult_ref, box_ref, pairs_ref, False)
-    add_pairs(lrecv_ref.at[1], boxes + 2 * plane, mult_ref, box_ref, pairs_ref, False)
+    add_pairs(lrecv_ref, 0, boxes, mult_ref, box_ref, pairs_ref, False)
     for copy in waits:
         copy.wait_send()
 
@@ -234,7 +241,7 @@
             pltpu.VMEM((2, depth + 4, 2 * (width_x + 4), comps), f32),
             pltpu.VMEM((2, edge_rows, comps), b16),
             pltpu.VMEM((2, edge_rows, comps), b16),
-            pltpu.VMEM((2, 2 * plane, comps), b16),
+            pltpu.VMEM((4 * plane, comps), b16),
             pltpu.VMEM((3, 8, comps), f32),
         ]
         + [pltpu.VMEM((count, 8, comps), f32) for count in counts]
@@ -242,8 +249,9 @@
             pltpu.VMEM((offsets, boxes, 128), b16),
             pltpu.VMEM((offsets, comps, comps), b16),
             pltpu.VMEM((5, 2, depth + 4, (width_x + 4) * width_y, comps), b16),
-            pltpu.VMEM((boxes, 5 * comps), b16),
             pltpu.VMEM((boxes, comps), f32),
+            pltpu.VMEM((128, comps), f32),
+            pltpu.VMEM((comps, 128), f32),
         ]
         + [pltpu.SemaphoreType.DMA((2, 2))] * 4
         + [pltpu.SemaphoreType.DMA((2, count)) for count in counts],
@@ -252,7 +260,7 @@
         ),
     )(
         pair_mult, pair_dens.reshape(1, pairs), pair_live.reshape(1, pairs), pair_box.reshape(1, pairs),
-        inter_mask.reshape(boxes, offsets), row_scale.T, col_scale, base, lattice,
+        inter_mask.reshape(boxes, offsets), row_scale, col_scale, base, lattice,
     )
     return (box_locals.reshape(depth, width_x, width_y, comps), pair_j.reshape(pairs))
 
@@ -263,16 +271,16 @@
     def step(index, carry):
         at = pl.ds(pl.multiple_of(index * 16, 16), 16)
         core = base_ref[at, :].astype(jnp.float32)
-        rows = rows_ref[at, :]
+        rows = rows_ref[at, :].astype(jnp.bfloat16)
         for entry in range(offsets):
-            scaled = core * rows[:, entry : entry + 1] * cols_ref[entry : entry + 1, :]
-            wide_ref[entry, at, :] = scaled.astype(jnp.bfloat16)
+            scaled = (core * cols_ref[entry : entry + 1, :]).astype(jnp.bfloat16)
+            wide_ref[entry, at, :] = scaled * rows[:, entry : entry + 1]
         return carry
 
     lax.fori_loop(0, comps // 16, step, 0)
 
 
-def expand_masks(mask_ref, wide_ref):
+def expand_masks(mask_ref, wide_ref, begin, end):
     offsets, boxes, lanes = wide_ref.shape
 
     def step(index, carry):
@@ -283,17 +291,18 @@
             wide_ref[entry, at, :] = wide.astype(jnp.bfloat16)
         return carry
 
-    lax.fori_loop(0, boxes // 32, step, 0)
-
-
-def shifted_copies(padded_ref, shifted_ref):
+    blocks = boxes // 32
+    lax.fori_loop(blocks * begin // 4, blocks * end // 4, step, 0)
+
+
+def shifted_copies(padded_ref, shifted_ref, moves):
     depth = padded_ref.shape[0]
     size_y = padded_ref.shape[2] - 4
     spread_x = padded_ref.shape[1]
     comps = padded_ref.shape[3]
 
     def step(level, carry):
-        for move in range(5):
+        for move in moves:
             part = padded_ref[level, :, move : move + size_y, :].astype(jnp.bfloat16)
             shifted_ref[move, 0, level] = part.reshape(spread_x * size_y, comps)
             part = padded_ref[level, 1 : spread_x - 1, move : move + size_y, :].astype(jnp.bfloat16)
@@ -305,7 +314,7 @@
     lax.fori_loop(0, depth, step, 0)
 
 
-def far_field(shifted_ref, gates_ref, wide_ref, total_ref, left_ref, sizes):
+def far_field(shifted_ref, gates_ref, wide_ref, total_ref, sizes):
     size_z, size_x, size_y = sizes
     rows = size_x * size_y
     boxes = size_z * rows
@@ -314,19 +323,18 @@
     def group(shift_z, shift_x, first, moves):
         even = (shift_x + 2) % 2
         start = pl.multiple_of(((shift_x + 2) // 2) * 2 * size_y, 2 * size_y)
+        left = []
         for place, move in enumerate(moves):
             source = shifted_ref[move + 2, even, pl.ds(shift_z + 2, size_z), pl.ds(start, rows), :]
             source = source.reshape(boxes, comps)
             gate = gates_ref[first + place]
             for half in range(comps // 128):
                 lanes = slice(half * 128, half * 128 + 128)
-                left_ref[:, place * comps + half * 128 : place * comps + half * 128 + 128] = (
-                    source[:, lanes] * gate
-                )
+                left.append(source[:, lanes] * gate)
         count = len(moves)
         operator = wide_ref[pl.ds(first, count)].reshape(count * comps, comps)
         total_ref[...] += jnp.dot(
-            left_ref[:, : count * comps], operator, preferred_element_type=jnp.float32
+            jnp.concatenate(left, axis=1), operator, preferred_element_type=jnp.float32
         )
 
     def outer(index, carry):

time: 58.9 us -> 51.4 us (0.87)
  Pallas kernels: 53.4 us -> 47.5 us
  local copies, waits for them, and re-layouts: 4.65 us -> 2.99 us
    pallas_call x1, Pallas kernels: 53.4 us -> 47.5 us  [per_device(): pl.pallas_call(functools.partial(fused_kernel, (depth, width_x, width_y))...]
    unnamed x3 -> x2, local copies, waits for them, and re-layouts: 4.65 us -> 2.99 us
where the time goes in v2:
time: 51.4 us; the launch traced here: 51.1 us
  Pallas kernels  47.5 us (92%)
  local copies, waits for them, and re-layouts  2.99 us (6%)
  between operations  0.64 us (1%)
    pallas_call x1, Pallas kernels, per_device(): pl.pallas_call(functools.partial(fused_kernel, (depth, width_x, width_y))...  47.5 us
    unnamed x2, local copies, waits for them, and re-layouts  2.99 us

profile of v2, /device:TPU:0, one launch (start us, length us, event | category | flops | bytes accessed | tf_op | source)
XLA Modules:
  0.0 51.1 jit_solution(15590300726878085557)
XLA Ops:
  0.6 47.5 %shard_map.104 = (bf16[512,256]{1,0:T(8,128)(2,1)}, f32[1,4096]{1,0:T(1,128)}) custom-call(bf16[4096,256]{1,0:T(8,128)(2,1)} %mult_ref.1, f32[1,4096]{1,0:T(1,128)} %bitcast.8, s32[1,4096]{1,0:T(1,128)} %bitcast.9, s32[1,4096]{1,0:T(1,128)} %bitcast.10, s32[512,98]{1,0:T(8,128)} %bitcast.6, f32[98,256]{1,0:T(8,128)} %rows_ref.1, f32[98,256]{1,0:T(8,128)} %cols_ref.1, ...), custom_call_target="tpu_custom_call" | custom-call | tf_op jit(solution)/shard_map/pallas_call | solution.py:227
  48.1 1.7 %copy.13 = bf16[8,8,8,256]{3,2,1,0:T(8,128)(2,1)} copy(bf16[8,8,8,256]{3,2,1,0:T(8,128)(2,1)} %bitcast.7) | data formatting | bytes 524288
  49.8 1.3 %copy.14 = f32[4096]{0:T(1024)} copy(f32[4096]{0:T(1024)} %bitcast.11) | data formatting | bytes 32768

commit v3 on v2

--- a/solution.py
+++ b/solution.py
@@ -21,16 +21,20 @@
     return listed
 
 
-def add_moments(mult_ref, dens_ref, live_ref, box_ref, near_ref):
-    near = near_ref.shape[0]
-    labels = lax.broadcasted_iota(jnp.int32, (near, PAIR_CHUNK), 0)
-    near_ref[...] = jnp.zeros_like(near_ref)
+def add_moments(mult_ref, dens_ref, live_ref, box_ref, near_ref, starts, length):
+    labels = jnp.concatenate(
+        [lax.broadcasted_iota(jnp.int32, (length, PAIR_CHUNK), 0) + start for start in starts], axis=0
+    )
+    for start in starts:
+        near_ref[start : start + length, :] = jnp.zeros((length, near_ref.shape[1]), jnp.float32)
 
     def step(index, carry):
         at = pl.ds(pl.multiple_of(index * PAIR_CHUNK, PAIR_CHUNK), PAIR_CHUNK)
         weight = dens_ref[:, at] * live_ref[:, at].astype(jnp.float32)
         selector = jnp.where(labels == box_ref[:, at], weight, 0.0).astype(jnp.bfloat16)
-        near_ref[...] += jnp.dot(selector, mult_ref[at, :], preferred_element_type=jnp.float32)
+        sums = jnp.dot(selector, mult_ref[at, :], preferred_element_type=jnp.float32)
+        for place, start in enumerate(starts):
+            near_ref[start : start + length, :] += sums[place * length : (place + 1) * length]
         return carry
 
     lax.fori_loop(0, mult_ref.shape[0] // PAIR_CHUNK, step, 0)
@@ -112,7 +116,8 @@
             )
             peers += 1
 
-    add_moments(mult_ref, dens_ref, live_ref, box_ref, near_ref)
+    pair_refs = (mult_ref, dens_ref, live_ref, box_ref, near_ref)
+    add_moments(*pair_refs, (0, size_z * plane), 4 * plane)
     zsend_ref[0] = near_ref[: 4 * plane].astype(jnp.bfloat16)
     zsend_ref[1] = near_ref[size_z * plane :].astype(jnp.bfloat16)
     pl.semaphore_wait(barrier, peers)
@@ -121,6 +126,7 @@
         send(zsend_ref.at[1], zrecv_ref.at[0], zsem, 1, neighbour("rows", 1)),
     ]
     zcopies = list(waits)
+    add_moments(*pair_refs, (4 * plane,), (size_z - 4) * plane)
     cells_ref[0] = jnp.broadcast_to(jnp.sum(near_ref[...], 0, keepdims=True), (8, comps))
     rcopies = share_cells("rows", cells_ref.at[0], cells_r, crsem)
     waits += rcopies
@@ -179,6 +185,8 @@
     waits += ccopies
     shifted_copies(padded_ref, shifted_ref, (2,))
     expand_masks(mask_ref, gates_ref, 2, 4)
+    total_ref[...] = jnp.zeros_like(total_ref)
+    far_field(shifted_ref, gates_ref, wide_ref, total_ref, sizes, True)
     for copy in ycopies:
         copy.wait_recv()
     pack_ref[...] = yrecv_ref[...].astype(jnp.float32).reshape(pack_ref.shape)
@@ -196,9 +204,8 @@
     term = jnp.dot(
         cell, lattice_ref[...], precision=lax.Precision.HIGHEST, preferred_element_type=jnp.float32
     )
-    total_ref[...] = jnp.broadcast_to(term[:1], total_ref.shape)
-    far_field(shifted_ref, gates_ref, wide_ref, total_ref, sizes)
-    out_ref[...] = total_ref[...].astype(jnp.bfloat16)
+    far_field(shifted_ref, gates_ref, wide_ref, total_ref, sizes, False)
+    out_ref[...] = (total_ref[...] + term[:1]).astype(jnp.bfloat16)
     boxes = size_z * plane
     lcopies = [
         send(out_ref.at[pl.ds(0, 2 * plane)], lrecv_ref.at[pl.ds(2 * plane, 2 * plane)], lsem, 0, neighbour("rows", -1)),
@@ -314,47 +321,49 @@
     lax.fori_loop(0, depth, step, 0)
 
 
-def far_field(shifted_ref, gates_ref, wide_ref, total_ref, sizes):
+def far_field(shifted_ref, gates_ref, wide_ref, total_ref, sizes, central):
     size_z, size_x, size_y = sizes
     rows = size_x * size_y
     boxes = size_z * rows
     comps = wide_ref.shape[1]
 
-    def group(shift_z, shift_x, first, moves):
+    def group(shift_z, shift_x, first, pairs):
         even = (shift_x + 2) % 2
         start = pl.multiple_of(((shift_x + 2) // 2) * 2 * size_y, 2 * size_y)
-        left = []
-        for place, move in enumerate(moves):
+        total = total_ref[...]
+        for place, move in pairs:
             source = shifted_ref[move + 2, even, pl.ds(shift_z + 2, size_z), pl.ds(start, rows), :]
             source = source.reshape(boxes, comps)
             gate = gates_ref[first + place]
-            for half in range(comps // 128):
-                lanes = slice(half * 128, half * 128 + 128)
-                left.append(source[:, lanes] * gate)
-        count = len(moves)
-        operator = wide_ref[pl.ds(first, count)].reshape(count * comps, comps)
-        total_ref[...] += jnp.dot(
-            jnp.concatenate(left, axis=1), operator, preferred_element_type=jnp.float32
-        )
+            left = [source[:, at : at + 128] * gate for at in range(0, comps, 128)]
+            total = total + jnp.dot(
+                jnp.concatenate(left, axis=1),
+                wide_ref[first + place],
+                preferred_element_type=jnp.float32,
+            )
+        total_ref[...] = total
+
+    ring_moves = ((2, 0),) if central else ((0, -2), (1, -1), (3, 1), (4, 2))
 
     def outer(index, carry):
         side, spot = index // 5, index % 5
-        group(side * 4 - 2, spot - 2, side * 73 + spot * 5, (-2, -1, 0, 1, 2))
+        group(side * 4 - 2, spot - 2, side * 73 + spot * 5, ring_moves)
         return carry
 
     def edge(index, carry):
         level, side = index // 2, index % 2
-        group(level - 1, side * 4 - 2, 25 + level * 16 + side * 11, (-2, -1, 0, 1, 2))
+        group(level - 1, side * 4 - 2, 25 + level * 16 + side * 11, ring_moves)
         return carry
 
     def inner(index, carry):
         level, spot = index // 3, index % 3
-        group(level - 1, spot - 1, 30 + level * 16 + spot * 2, (-2, 2))
+        group(level - 1, spot - 1, 30 + level * 16 + spot * 2, ((0, -2), (1, 2)))
         return carry
 
     lax.fori_loop(0, 10, outer, 0)
     lax.fori_loop(0, 6, edge, 0)
-    lax.fori_loop(0, 9, inner, 0)
+    if not central:
+        lax.fori_loop(0, 9, inner, 0)
 
 
 def solution(mesh):

time: 51.4 us -> 50.6 us (0.984)
  Pallas kernels: 47.5 us -> 46.7 us
    pallas_call x1, Pallas kernels: 47.5 us -> 46.7 us  [per_device(): pl.pallas_call(functools.partial(fused_kernel, (depth, width_x, width_y))...]
where the time goes in v3:
time: 50.6 us; the launch traced here: 50.4 us
  Pallas kernels  46.7 us (92%)
  local copies, waits for them, and re-layouts  2.99 us (6%)
  between operations  0.64 us (1%)
    pallas_call x1, Pallas kernels, per_device(): pl.pallas_call(functools.partial(fused_kernel, (depth, width_x, width_y))...  46.7 us
    unnamed x2, local copies, waits for them, and re-layouts  2.99 us

profile of v3, /device:TPU:0, one launch (start us, length us, event | category | flops | bytes accessed | tf_op | source)
XLA Modules:
  0.0 50.4 jit_solution(11644703709747294746)
XLA Ops:
  0.6 46.7 %shard_map.104 = (bf16[512,256]{1,0:T(8,128)(2,1)}, f32[1,4096]{1,0:T(1,128)}) custom-call(bf16[4096,256]{1,0:T(8,128)(2,1)} %mult_ref.1, f32[1,4096]{1,0:T(1,128)} %bitcast.8, s32[1,4096]{1,0:T(1,128)} %bitcast.9, s32[1,4096]{1,0:T(1,128)} %bitcast.10, s32[512,98]{1,0:T(8,128)} %bitcast.6, f32[98,256]{1,0:T(8,128)} %rows_ref.1, f32[98,256]{1,0:T(8,128)} %cols_ref.1, ...), custom_call_target="tpu_custom_call" | custom-call | tf_op jit(solution)/shard_map/pallas_call | solution.py:234
  47.4 1.7 %copy.13 = bf16[8,8,8,256]{3,2,1,0:T(8,128)(2,1)} copy(bf16[8,8,8,256]{3,2,1,0:T(8,128)(2,1)} %bitcast.7) | data formatting | bytes 524288
  49.0 1.3 %copy.14 = f32[4096]{0:T(1024)} copy(f32[4096]{0:T(1024)} %bitcast.11) | data formatting | bytes 32768
